TPU v7x, 32 devices: a whole 2x2x4 slice. The times are simulated.
32 devices in a mesh: wide: 8 (over y, x, core), narrow: 4 (over z).
Axes of the slice: x: 2, y: 2, z: 4, core: 2. Of those that a mesh axis runs over, the one named last changes fastest.
Arguments:
- tracers: float32 [4, 221, 65536], P(None, None, ('wide', 'narrow')), may hold values from -6 to 6
- column_rate: float32 [65536], P(('wide', 'narrow')), may hold values from 0.25 to 2
- loss_rate: float32 [221], replicated, may hold values from 0.05 to 3
- coupling: bfloat16 [221, 221], replicated, may hold values from -0.375 to 0.375
- phys_index: int32 [65536], P(('wide', 'narrow')), may hold values from 0 to 65535, as said below
- iter_count: int32 [65536], P(('wide', 'narrow')), may hold values from 2 to 12, as said below
Outputs:
- updated: float32 [4, 221, 65536], P(None, None, ('wide', 'narrow'))
Inputs may be any that keep to these rules, and one draw needn't show every extreme that they name: A permutation of the columns: column c goes to the device phys_index[c] // 2048 (devices in wide-major order) at slot phys_index[c] % 2048. A device at wide index w sends columns only to devices at wide indices w - 1 to w + 2, with wrap. For each wide step and narrow step (with wrap) every device sends the same number of columns to the device that many steps further on; at most 256, and exactly 256 for some pair of steps. The columns from one device to one device fill a contiguous range of slots. `iter_count`: columns whose physics device lies in 4 consecutive wide indices (with wrap) take 12 // 2 to 12 substeps, the others 2 to 3.
All inputs are finite; a program needn't handle non-finite values.
Results may differ from a plain program's by a relative error of at most 0.00072.
Values sent between devices are 32-bit elements; how exact they have to be, the bound alone decides.
No kernel may reach another device: no remote copies, remote signals or barrier semaphores. Data moves between devices by JAX's collectives and lax.ppermute only.
A program may use at most 128 MiB of HBM per device.

v0:
```python
import functools

import jax
import jax.numpy as jnp
from jax import lax
from jax.experimental import pallas as pl
from jax.experimental.pallas import tpu as pltpu
from jax.sharding import PartitionSpec as P

WIN = 4
MAXIT = 12
LANES = 128
SORT_COLUMNS = 256
INT_ROWS = 256
UNIT = 8
VMEM = 64 * 1024 * 1024 - 256 * 1024


def from_behind(value, axis, steps):
    count = lax.axis_size(axis)
    pairs = [(source, (source + steps) % count) for source in range(count)]
    return lax.ppermute(value, axis, pairs)


def log2(value):
    bits = value.bit_length() - 1
    assert 1 << bits == value
    return bits


def span_of(group, groups, tiles):
    return pl.ds(pl.multiple_of(group * 8 * tiles, 8), groups * 8 * tiles)


def sort_kernel(sizes, cuts, targets, early, *refs):
    species, levels, columns, tiles, wide_count, narrow_count, pair_total = sizes
    turn_ref, wide_ref, sorted_ref = refs[-4:-1]
    sem_ref = refs[-1]
    if early:
        phys_ref, rate_ref, count_ref, tracers_ref, table_ref, pos_ref = refs[:6]
        cut_refs = refs[6:6 + targets]
        at_ref, table_smem, place_sem = refs[6 + targets:9 + targets]
    else:
        phys_ref, rate_ref, count_ref, tracers_ref, table_smem, at_ref = refs[:6]
        cut_refs = refs[6:6 + targets]
    step = pl.program_id(0)
    lanes = tiles * LANES
    real = species * levels

    def find_places():
        phys = phys_ref[...]
        target = lax.shift_right_logical(phys, log2(columns))
        slot = phys & (columns - 1)
        wide_step = lax.shift_right_logical(target, log2(narrow_count)) - lax.axis_index("wide")
        wide_step = (wide_step + 1) & (wide_count - 1)
        narrow_step = ((target & (narrow_count - 1)) - lax.axis_index("narrow")) & (narrow_count - 1)
        pair = narrow_step * WIN + wide_step
        member = pair == lax.broadcasted_iota(jnp.int32, (pair_total, columns), 0)
        counts = jnp.sum(jnp.where(member, 1.0, 0.0), axis=1, keepdims=True)
        slot_f = slot.astype(jnp.float32)
        starts = jnp.min(jnp.where(member, slot_f, float(columns)), axis=1, keepdims=True)
        groups = lax.shift_right_logical(counts.astype(jnp.int32) + 7, 3).astype(jnp.float32)
        lane = lax.broadcasted_iota(jnp.int32, (pair_total, LANES), 1)
        row = lax.broadcasted_iota(jnp.int32, (pair_total, LANES), 0)

        def across(value):
            return jnp.sum(jnp.where(lane == row, value, 0.0), axis=0, keepdims=True)

        groups_t = across(groups)
        base = jnp.sum(jnp.where(lane < row, groups_t, 0.0), axis=1, keepdims=True)
        section = row & -WIN
        inner = base - jnp.sum(jnp.where(lane < section, groups_t, 0.0), axis=1, keepdims=True)
        same = (lane & -WIN) == section
        in_step = jnp.sum(jnp.where(same, groups_t, 0.0), axis=1, keepdims=True)
        pos = slot_f + jnp.sum(jnp.where(member, base * 8.0 - starts, 0.0), axis=0, keepdims=True)
        pos_ref[...] = pos.astype(jnp.int32)
        pltpu.make_async_copy(pos_ref, at_ref, place_sem.at[0]).start()
        table_ref[...] = jnp.zeros_like(table_ref)
        for at, value in enumerate((counts, base, inner, in_step)):
            table_ref[at:at + 1, :] = across(value).astype(jnp.int32)
        pltpu.make_async_copy(table_ref, table_smem, place_sem.at[1]).start()

    if early:
        pl.when(step == 0)(find_places)
    block = tracers_ref.shape[2]
    begin = step * block
    in_group = lax.broadcasted_iota(jnp.int32, (8, LANES), 0)
    for half in range(block // LANES):
        span = slice(half * LANES, (half + 1) * LANES)
        at = pl.ds(pl.multiple_of(begin + half * LANES, LANES), LANES)
        turn_ref[lanes - 16:lanes, :] = jnp.zeros((16, LANES), jnp.float32)
        turn_ref[0:real, :] = tracers_ref[:, :, span].reshape(real, LANES)
        extra = jnp.where(in_group == 5, (phys_ref[:, at] & (columns - 1)).astype(jnp.float32), 0.0)
        extra = jnp.where(in_group == 6, rate_ref[:, at], extra)
        extra = jnp.where(in_group == 7, count_ref[:, at].astype(jnp.float32), extra)
        turn_ref[lanes - 8:lanes, :] = extra
        for tile in range(tiles):
            wide_ref[half, pl.ds(tile, LANES, stride=8), :] = turn_ref[
                tile * LANES:(tile + 1) * LANES, :
            ].T

        if early and half == 0:
            @pl.when(step == 0)
            def _():
                pltpu.make_async_copy(pos_ref, at_ref, place_sem.at[0]).wait()
                pltpu.make_async_copy(table_ref, table_smem, place_sem.at[1]).wait()

        for column in range(LANES):
            to = at_ref[0, begin + half * LANES + column] * tiles
            sorted_ref[pl.ds(to, tiles), :] = wide_ref[half, column * 8:column * 8 + tiles, :]

    @pl.when(step == pl.num_programs(0) - 1)
    def _():
        copies = []
        for index, (target, to, begin, size, valid) in enumerate(cuts):
            begin = begin(table_smem)
            valid = jnp.clip(valid(table_smem), 0, size)
            copy = pltpu.make_async_copy(
                sorted_ref.at[span_of(begin, size, tiles)],
                cut_refs[target].at[span_of(to, size, tiles)], sem_ref.at[index],
            )
            pl.when(valid > 0)(copy.start)
            copies.append((valid > 0, copy))
        wait_all(copies)


def start_arrival(refs, sem_ref, room_ref, in_step, static, tiles):
    waits = []
    quarter = static // 4
    for part in range(4):
        span = span_of(part * quarter, quarter, tiles)
        copy = pltpu.make_async_copy(refs[0].at[span], room_ref.at[span], sem_ref.at[part])
        copy.start()
        waits.append((None, copy))
    copy = pltpu.make_async_copy(
        refs[1], room_ref.at[pl.ds(static * 8 * tiles, refs[1].shape[0])], sem_ref.at[4]
    )
    pl.when(in_step > static)(copy.start)
    waits.append((in_step > static, copy))
    return waits


def wait_all(waits):
    for wanted, copy in waits:
        if wanted is None:
            copy.wait()
        else:
            pl.when(wanted)(copy.wait)


def integrate_block(sizes, room_ref, first, valid, loss_ref, coupling_ref,
                    turn_ref, y_ref, inverse_ref):
    levels, pad, tiles = sizes
    halves = INT_ROWS // LANES
    lanes = tiles * LANES
    first = pl.multiple_of(first * 8 * tiles, 8)
    for half in range(halves):
        begin = first + half * LANES * tiles
        for tile in range(tiles):
            block = room_ref[pl.ds(begin + tile, LANES, stride=tiles), :]
            turn_ref[half, tile * LANES:(tile + 1) * LANES, :] = block.T
        for level in range(levels):
            y_ref[level, :, half * LANES:(half + 1) * LANES] = turn_ref[
                half, pl.ds(level, pad, stride=levels), :
            ]
    rate = jnp.concatenate(
        [turn_ref[half, lanes - 2:lanes - 1, :] for half in range(halves)], axis=1
    )
    count = jnp.concatenate(
        [turn_ref[half, lanes - 1:lanes, :] for half in range(halves)], axis=1
    )
    lane = lax.broadcasted_iota(jnp.int32, (1, INT_ROWS), 1)
    count = jnp.where((lane < valid) & (count <= MAXIT), count, 0.0)
    step_len = rate / jnp.maximum(count, 1.0)
    inverse_ref[...] = 1.0 / (1.0 + step_len * loss_ref[...])
    last = jnp.max(count).astype(jnp.int32)

    def advance(k, carry):
        active = k.astype(jnp.float32) < count

        def one_level(level, inner):
            y = y_ref[level]
            squashed = jnp.tanh(y).astype(jnp.bfloat16)
            produced = jnp.dot(coupling_ref[...], squashed, preferred_element_type=jnp.float32)
            y_ref[level] = jnp.where(active, (y + step_len * produced) * inverse_ref[...], y)
            return inner

        for level in range(levels):
            one_level(level, 0)
        return carry

    lax.fori_loop(0, last, advance, 0)
    for half in range(halves):
        begin = first + half * LANES * tiles
        for level in range(levels):
            turn_ref[half, pl.ds(level, pad, stride=levels), :] = y_ref[
                level, :, half * LANES:(half + 1) * LANES
            ]
        for tile in range(tiles):
            block = turn_ref[half, tile * LANES:(tile + 1) * LANES, :]
            room_ref[pl.ds(begin + tile, LANES, stride=tiles), :] = block.T


def integrate_kernel(sizes, plan, table_ref, loss_ref, coupling_ref, *refs):
    loads, merges, blocks, stores, operands = plan
    tiles = sizes[2]
    sources = refs[:operands]
    results = refs[operands:operands + len(stores)]
    room_ref, turn_ref, y_ref, inverse_ref, rows_ref, sem_ref, out_sem = refs[
        operands + len(stores):
    ]
    copies = []
    for index, (source, begin, groups, to) in enumerate(loads):
        ref = sources[source]
        if begin is not None:
            ref = ref.at[span_of(begin(table_ref), groups, tiles)]
        copies.append(pltpu.make_async_copy(
            ref, room_ref.at[span_of(to, groups, tiles)], sem_ref.at[index]
        ))
    for copy in copies:
        copy.start()
    for copy in copies:
        copy.wait()
    for begin, groups, to in merges:
        to = to(table_ref)

        def move(group, carry):
            room_ref[span_of(to + group, 1, tiles), :] = room_ref[
                span_of(begin + group, 1, tiles), :
            ]
            return carry

        lax.fori_loop(0, groups(table_ref), move, 0)
    for index, (begin, rows) in enumerate(blocks):
        rows_ref[0, index] = jnp.int32(begin)
        rows_ref[1, index] = rows(table_ref)

    def one_block(index, carry):
        valid = rows_ref[1, index]

        @pl.when(valid > 0)
        def _():
            integrate_block(sizes, room_ref, rows_ref[0, index], valid, loss_ref, coupling_ref,
                            turn_ref, y_ref, inverse_ref)

        return carry

    lax.fori_loop(0, len(blocks), one_block, 0)
    copies = []
    for index, (begin, groups) in enumerate(stores):
        copies.append(pltpu.make_async_copy(
            room_ref.at[span_of(begin(table_ref), groups, tiles)], results[index],
            out_sem.at[index],
        ))
    for copy in copies:
        copy.start()
    for copy in copies:
        copy.wait()


def cut_kernel(static, tiles, piece, step, table_ref, *refs):
    pieces = refs[2:2 + WIN]
    room_ref, sem_ref, out_sem = refs[2 + WIN:]
    wait_all(start_arrival(refs[:2], sem_ref, room_ref, table_ref[3, step * WIN], static, tiles))
    copies = []
    quarter = piece // 4
    for at in range(WIN):
        begin = table_ref[2, step * WIN + at]
        for part in range(4):
            wanted = table_ref[0, step * WIN + at] > part * quarter * 8
            copy = pltpu.make_async_copy(
                room_ref.at[span_of(begin + part * quarter, quarter, tiles)],
                pieces[at].at[span_of(part * quarter, quarter, tiles)], out_sem.at[part, at],
            )
            pl.when(wanted)(copy.start)
            copies.append((wanted, copy))
    wait_all(copies)


def finish_kernel(sizes, table_ref, *refs):
    species, levels, columns, tiles, static, piece, narrow_count, begins = sizes
    pair_total = narrow_count * WIN
    whole_pieces = pair_total - WIN
    (out_ref, piece_ref, room_ref, placed_ref, whole_ref, sem_ref, room_sem,
     out_sem) = refs[-8:]
    copies = []
    quarter = piece // 4
    for pair in range(whole_pieces):
        parts = []
        for part in range(4):
            copy = pltpu.make_async_copy(
                refs[pair].at[span_of(begins[pair] + part * quarter, quarter, tiles)],
                piece_ref.at[pair, span_of(part * quarter, quarter, tiles)],
                sem_ref.at[part, pair],
            )
            wanted = table_ref[0, pair] > part * quarter * 8
            pl.when(wanted)(copy.start)
            parts.append((wanted, copy))
        copies.append(parts)
    waits = start_arrival(refs[whole_pieces:whole_pieces + 2], room_sem, room_ref,
                          table_ref[3, whole_pieces], static, tiles)
    lane = lax.broadcasted_iota(jnp.int32, (1, LANES), 1)
    in_group = lax.broadcasted_iota(jnp.int32, (8, LANES), 0)
    for pair in range(pair_total):
        if pair < whole_pieces:
            wait_all(copies[pair])
            held = piece_ref.at[pair]
            begin = 0
        else:
            if pair == whole_pieces:
                wait_all(waits)
            held = room_ref
            begin = pl.multiple_of(table_ref[2, pair] * 8 * tiles, 8)
        count = table_ref[0, pair]
        first = held[pl.ds(begin + tiles - 1, 1), :]
        start = jnp.max(jnp.where(lane == LANES - 3, first, 0.0)).astype(jnp.int32)
        start = jnp.clip(start, 0, columns - 1) * tiles
        full = lax.shift_right_logical(count, 3)

        def move(group, carry):
            for row in range(0, 8 * tiles, 8):
                at = group * 8 * tiles + row
                placed_ref[pl.ds(start + at, 8), :] = held[pl.ds(pl.multiple_of(begin + at, 8), 8), :]
            return carry

        lax.fori_loop(0, full, move, 0)

        @pl.when((count & 7) > 0)
        def _():
            for row in range(0, 8 * tiles, 8):
                at = full * 8 * tiles + row
                to = pl.ds(start + at, 8)
                placed_ref[to, :] = jnp.where(
                    in_group + row < (count & 7) * tiles,
                    held[pl.ds(pl.multiple_of(begin + at, 8), 8), :], placed_ref[to, :],
                )

    per_tile = LANES // levels
    for part in range(columns // LANES):
        at = slice(part * LANES, (part + 1) * LANES)
        for tile in range(tiles):
            block = placed_ref[pl.ds(part * LANES * tiles + tile, LANES, stride=tiles), :]
            block = block.T.reshape(per_tile, levels, LANES)
            keep = min(per_tile, species - tile * per_tile)
            whole_ref[tile * per_tile:tile * per_tile + keep, :, at] = block[:keep]
        pltpu.make_async_copy(whole_ref.at[:, :, at], out_ref.at[:, :, at], out_sem.at[part]).start()
    for part in range(columns // LANES):
        at = slice(part * LANES, (part + 1) * LANES)
        pltpu.make_async_copy(whole_ref.at[:, :, at], out_ref.at[:, :, at], out_sem.at[part]).wait()


def local(tracers, column_rate, loss_rate, coupling, phys_index, iter_count):
    levels, species, columns = tracers.shape
    wide_count = lax.axis_size("wide")
    narrow_count = lax.axis_size("narrow")
    pair_total = WIN * narrow_count
    room = 2 * columns // pair_total
    piece = room // 8
    pad = -(-species // 8) * 8
    while levels * pad % LANES or levels * (pad - species) < 8:
        pad += 8
    tiles = levels * pad // LANES
    mean = columns // narrow_count // 8
    full = pl.BlockSpec(memory_space=pltpu.VMEM)
    smem = pl.BlockSpec(memory_space=pltpu.SMEM)
    hbm = pl.BlockSpec(memory_space=pltpu.HBM)
    last = narrow_count - 1
    moving = [at for at in range(WIN) if at != 1]
    order = [narrow_count // 2]
    order += [step for step in range(1, last) if step not in order] + [last]
    statics = {step: mean - UNIT if step == order[0] else mean for step in order}
    most = WIN * piece

    params = pltpu.CompilerParams(vmem_limit_bytes=VMEM)

    def rows_type(groups):
        return jax.ShapeDtypeStruct((groups * 8 * tiles, LANES), jnp.float32)

    def room_type(groups):
        return pltpu.VMEM((groups * 8 * tiles, LANES), jnp.float32)

    def entry(row, step, at=0):
        return lambda table: table[row, step * WIN + at]

    def over(step):
        return lambda table: entry(1, step)(table) + statics[step]

    def groups_of(step, at):
        return lambda table: lax.shift_right_logical(table[0, step * WIN + at] + 7, 3)

    def groups_over(step):
        return lambda table: table[3, step * WIN] - statics[step]

    def pair_cuts(target, at):
        return [
            (target, part * piece + half,
             lambda table, step=step, half=half: entry(1, step, at)(table) + half, piece // 2,
             lambda table, step=step, half=half: groups_of(step, at)(table) - half)
            for part, step in enumerate((0, last)) for half in range(0, piece, piece // 2)
        ]

    def sort(cuts, target_sizes, early, known):
        known_types = [
            jax.ShapeDtypeStruct((8, LANES), jnp.int32),
            jax.ShapeDtypeStruct((1, columns), jnp.int32),
        ]
        groups = columns // 8 + pair_total + most
        return pl.pallas_call(
            functools.partial(
                sort_kernel,
                (species, levels, columns, tiles, wide_count, narrow_count, pair_total),
                cuts, len(target_sizes), early,
            ),
            grid=(columns // SORT_COLUMNS,),
            in_specs=[full, full, full,
                      pl.BlockSpec((species, levels, SORT_COLUMNS), lambda at: (0, 0, at))]
            + [smem] * len(known),
            out_specs=([full, full] if early else []) + [hbm] * len(target_sizes),
            out_shape=(known_types if early else []) + [rows_type(size) for size in target_sizes],
            scratch_shapes=([
                pltpu.SMEM((1, columns), jnp.int32), pltpu.SMEM((8, LANES), jnp.int32),
                pltpu.SemaphoreType.DMA((2,)),
            ] if early else []) + [
                pltpu.VMEM((tiles * LANES, LANES), jnp.float32),
                pltpu.VMEM((SORT_COLUMNS // LANES, LANES * 8, LANES), jnp.float32),
                room_type(groups),
                pltpu.SemaphoreType.DMA((len(cuts),)),
            ],
            compiler_params=params,
            name="sort_columns" if early else "sort_later_columns",
        )(
            phys_index.reshape(1, columns),
            column_rate.reshape(1, columns),
            iter_count.reshape(1, columns),
            tracers.transpose(1, 0, 2),
            *known,
        )

    first_static = statics[order[0]]
    cuts = [(0, 0, entry(1, order[0]), first_static, entry(3, order[0]))]
    for index, at in enumerate(moving):
        cuts += pair_cuts(1 + index, at)
    table, places, *first = sort(
        cuts, [first_static] + [2 * piece] * len(moving), True, ()
    )
    cuts = [(0, 0, over(order[0]), most - first_static, groups_over(order[0]))]
    cuts += pair_cuts(1, 1)
    for index, step in enumerate(order[1:-1]):
        rest = most - statics[step]
        cuts.append((2 + index, 0, entry(1, step), statics[step], entry(3, step)))
        cuts.append((2 + index, statics[step], over(step), rest, groups_over(step)))
    first_rest, local_rows, *raw = sort(
        cuts, [most - first_static, 2 * piece] + [most] * (len(order) - 2), False, (table, places)
    )
    raw_groups = dict(zip(order[1:-1], raw))
    units = [
        (jnp.maximum(table[3, step * WIN] - statics[step], 0) + UNIT - 1) // UNIT
        for step in order
    ]
    loss_pad = jnp.pad(loss_rate, (0, pad - species)).reshape(pad, 1)
    coupling_pad = jnp.pad(coupling, ((0, pad - species), (0, pad - species)))
    block = INT_ROWS // 8

    def integrate(table, operands, loads, merges, blocks, stores):
        groups = max([to + size for _, _, size, to in loads] + [begin + block for begin, _ in blocks])
        groups += piece
        return pl.pallas_call(
            functools.partial(
                integrate_kernel, (levels, pad, tiles),
                (loads, merges, blocks, stores, len(operands)),
            ),
            in_specs=[smem, full, full] + [hbm] * len(operands),
            out_specs=[hbm] * len(stores),
            out_shape=[rows_type(size) for _, size in stores],
            scratch_shapes=[
                room_type(groups),
                pltpu.VMEM((INT_ROWS // LANES, tiles * LANES, LANES), jnp.float32),
                pltpu.VMEM((levels, pad, INT_ROWS), jnp.float32),
                pltpu.VMEM((pad, INT_ROWS), jnp.float32),
                pltpu.SMEM((2, LANES), jnp.int32),
                pltpu.SemaphoreType.DMA((len(loads),)),
                pltpu.SemaphoreType.DMA((len(stores),)),
            ],
            compiler_params=params,
            name="integrate_columns",
        )(table, loss_pad, coupling_pad, *operands)

    def rows_of(step, at=0):
        return entry(0, step, at)

    def group_blocks(begin, step):
        return [
            (begin + part * block,
             lambda table, part=part: table[3, step * WIN] * 8 - part * INT_ROWS)
            for part in range(most // block)
        ]

    def here(begin):
        return lambda table: jnp.int32(begin)

    def step_over(step, units, rest):
        def leaf(units, rest):
            if units == 0:
                return rest
            got = from_behind(rest[:units * UNIT * 8 * tiles], "narrow", step)
            return lax.dynamic_update_slice(rest, got, (0, 0))

        leaves = [functools.partial(leaf, count) for count in range((most - statics[step]) // UNIT + 1)]
        return lax.switch(units, leaves, rest)

    pieces = {}
    outgoing = [first[0], first_rest]
    wide_now = first[1:]
    keys_now = [[(at, 0), (at, last)] for at in moving]
    static_part = from_behind(outgoing[0], "narrow", order[0])
    wide_got = [from_behind(value, "wide", at - 1) for value, at in zip(wide_now, moving)]
    table_then = table
    for phase, step in enumerate(order):
        static = statics[step]
        operands, loads, merges, blocks, stores, named = [], [], [], [], [], []
        used = 0
        if phase + 1 < len(order):
            coming = order[phase + 1]
            if coming == last:
                operands += [pieces[at, last][0] for at in moving] + [local_rows]
                for index, at in enumerate(moving):
                    loads.append((index, here(pieces[at, last][1]), piece, most + at * piece))
                loads.append((len(moving), here(piece), piece, most + piece))
                for at in range(WIN):
                    merges.append(
                        (most + at * piece, groups_of(last, at), entry(2, last, at))
                    )
                used = most + WIN * piece
            else:
                operands.append(raw_groups[coming])
                loads.append((0, None, most, 0))
                used = most
            blocks += group_blocks(0, coming)
            stores += [(here(0), statics[coming]), (here(statics[coming]), most - statics[coming])]
        extra = []
        if phase == 0:
            extra.append(((1, 0), (local_rows, 0)))
        if phase == 1:
            extra += [((at, 0), pieces[at, 0]) for at in moving]
        if phase == 2:
            extra += [((at, order[0]), pieces[at, order[0]]) for at in range(WIN)]
        used = -(-used // block) * block
        for key, value in extra:
            operands.append(value[0])
            loads.append((len(operands) - 1, here(value[1]), piece, used))
            blocks.append((used, rows_of(key[1], key[0])))
            stores.append((here(used), piece))
            named.append(key)
            used += block
        if stores:
            results = integrate(table_then, operands, loads, merges, blocks, stores)
        else:
            results = []
        rest = outgoing[1]
        if phase == 0:
            static_part, results, rest, units = lax.optimization_barrier(
                (static_part, results, rest, units)
            )
        else:
            static_part, results, rest = lax.optimization_barrier((static_part, results, rest))
        done = {key: (value, 0) for key, value in zip(named, results[len(results) - len(named):])}
        outgoing = results[:len(results) - len(named)]
        arrived = [static_part, step_over(step, units[phase], rest)]
        if step != last:
            arrived, outgoing = lax.optimization_barrier((arrived, outgoing))
            static_part = from_behind(outgoing[0], "narrow", order[phase + 1])
        if step != last:
            cut = pl.pallas_call(
                functools.partial(cut_kernel, static, tiles, piece, step),
                in_specs=[smem] + [hbm] * len(arrived),
                out_specs=[hbm] * WIN,
                out_shape=[rows_type(piece)] * WIN,
                scratch_shapes=[
                    room_type(most + piece),
                    pltpu.SemaphoreType.DMA((5,)),
                    pltpu.SemaphoreType.DMA((4, WIN)),
                ],
                compiler_params=params,
                name="cut_pieces",
            )(table, *arrived)
            cut, wide_got, table_then = lax.optimization_barrier((cut, wide_got, table))
        for keys, value in zip(keys_now, wide_got):
            pieces.update({key: (value, part * piece) for part, key in enumerate(keys)})
        pieces.update(done)
        if step != last:
            pieces[1, step] = (cut[1], 0)
            keys_now = [[(at, step)] for at in moving]
            wide_got = [from_behind(cut[at], "wide", at - 1) for at in moving]

    held = [pieces[at, step] for step in range(last) for at in range(WIN)]
    buffers = [value for value, _ in held] + arrived
    updated = pl.pallas_call(
        functools.partial(
            finish_kernel,
            (species, levels, columns, tiles, static, piece, narrow_count,
             [begin for _, begin in held]),
        ),
        in_specs=[smem] + [hbm] * len(buffers),
        out_specs=hbm,
        out_shape=jax.ShapeDtypeStruct((species, levels, columns), jnp.float32),
        scratch_shapes=[
            pltpu.VMEM((pair_total - WIN, piece * 8 * tiles, LANES), jnp.float32),
            room_type(most + piece),
            room_type(columns // 8 + 1),
            pltpu.VMEM((species, levels, columns), jnp.float32),
            pltpu.SemaphoreType.DMA((4, pair_total)),
            pltpu.SemaphoreType.DMA((5,)),
            pltpu.SemaphoreType.DMA((columns // LANES,)),
        ],
        compiler_params=params,
        name="place_columns",
    )(table, *buffers)
    return updated.transpose(1, 0, 2)


def solution(mesh):
    placed = (
        P(None, None, ("wide", "narrow")),
        P(("wide", "narrow")),
        P(),
        P(),
        P(("wide", "narrow")),
        P(("wide", "narrow")),
    )
    return jax.shard_map(
        local,
        mesh=mesh,
        in_specs=placed,
        out_specs=P(None, None, ("wide", "narrow")),
        check_vma=False,
    )
```

profile of v0, /device:TPU:0, one launch (start us, length us, event | category | flops | bytes accessed | tf_op | source)
XLA Modules:
  0.0 254.5 jit_solution(17018912041953317838)
XLA Ops:
  0.0 11.1 %sort_columns.1 = (s32[8,128]{1,0:T(8,128)}, s32[1,2048]{1,0:T(1,128)}, f32[3136,128]{1,0:T(8,128)}, f32[3584,128]{1,0:T(8,128)}, f32[3584,128]{1,0:T(8,128)}, /*index=5*/f32[3584,128]{1,0:T(8,128)}) custom-call(s32[1,2048]{1,0:T(1,128)} %bitcast.11, f32[1,2048]{1,0:T(1,128)} %bitcast.13, s32[1,2048]{1,0:T(1,128)} %bitcast.15, f32[221,4,2048]{2,1,0:T(4,128)} %bitcast.9), custom_call_target="tpu_custom_call" | custom-call | tf_op jit(solution)/shard_map/sort_columns/pallas_call | solution.py:408
  11.1 4.1 %collective-permute-start.25 = (f32[3136,128]{1,0:T(8,128)}, f32[3136,128]{1,0:T(8,128)}, u32[]{:S(2)}, u32[]{:S(2)}) collective-permute-start(f32[3136,128]{1,0:T(8,128)} %get-tuple-element.139), channel_id=1, source_target_pairs={{0,2},{1,3},{2,0},{3,1},{4,6},{5,7},{6,4},{7,5},{8,10},{9,11},{10,... | collective-permute-start | bytes 4816904 | tf_op jit(solution)/shard_map/ppermute | solution.py:22
  15.2 1.6 collective-permute-start.27
  17.2 1.5 fusion
  21.4 10.6 %sort_later_columns.1 = (f32[4032,128]{1,0:T(8,128)}, f32[3584,128]{1,0:T(8,128)}, f32[7168,128]{1,0:T(8,128)}) custom-call(s32[1,2048]{1,0:T(1,128)} %bitcast.12, f32[1,2048]{1,0:T(1,128)} %bitcast.14, s32[1,2048]{1,0:T(1,128)} %bitcast.16, f32[221,4,2048]{2,1,0:T(4,128)} %bitcast.10, s32[8,128]{1,0:T(8,128)} %get-tuple-element.195.refs_4_.table_ref, ...), custom_call_target="tpu_custom_call" | custom-call | tf_op jit(solution)/shard_map/sort_later_columns/pallas_call | solution.py:408
  32.7 21.6 %integrate_columns.3 = (f32[3584,128]{1,0:T(8,128)}, f32[3584,128]{1,0:T(8,128)}, f32[1792,128]{1,0:T(8,128)}) custom-call(s32[8,128]{1,0:T(8,128)} %get-tuple-element.195.refs_4_.table_ref, f32[224,1]{1,0:T(8,128)} %copy.7.loss_ref, bf16[224,224]{1,0:T(8,128)(2,1)} %pad.9.coupling_ref, f32[7168,128]{1,0:T(8,128)} %get-tuple-element.141.refs_0_, ...), custom_call_target="tpu_custom_call" | custom-call | tf_op jit(solution)/shard_map/integrate_columns/pallas_call | solution.py:467
  54.3 30.7 %collective-permute-done.25.refs_0_ = f32[3136,128]{1,0:T(8,128)} collective-permute-done((f32[3136,128]{1,0:T(8,128)}, f32[3136,128]{1,0:T(8,128)}, u32[]{:S(2)}, u32[]{:S(2)}) %collective-permute-start.25) | collective-permute-done | bytes 1605664 | tf_op jit(solution)/shard_map/ppermute | solution.py:22
  85.0 44.4 %conditional.3 = (f32[4032,128]{1,0:T(8,128)}) conditional(s32[]{:T(128)} %clamp.9, f32[4032,128]{1,0:T(8,128)} %get-tuple-element.149, f32[4032,128]{1,0:T(8,128)} %get-tuple-element.149, f32[4032,128]{1,0:T(8,128)} %get-tuple-element.149, f32[4032,128]{1,0:T(8,128)} %get-tuple-element.149, ...), branch_computations={%region_0.1_spmd, %region_1.2_spmd, %region_2.3_spmd, %region_3.4_... | conditional | bytes 31195240 | solution.py:509
  85.0 1.2 slice.53
  86.4 42.1 %collective-permute-done.6 = f32[1792,128]{1,0:T(8,128)S(1)} collective-permute-done((f32[1792,128]{1,0:T(8,128)S(1)}, f32[1792,128]{1,0:T(8,128)S(1)}, u32[]{:S(2)}, u32[]{:S(2)}) %collective-permute-start.6) | collective-permute-done | bytes 917536 | tf_op jit(solution)/shard_map/cond/branch_4_fun/ppermute | solution.py:22
  129.5 4.5 %cut_pieces.2 = (f32[1792,128]{1,0:T(8,128)}, f32[1792,128]{1,0:T(8,128)}, f32[1792,128]{1,0:T(8,128)}, f32[1792,128]{1,0:T(8,128)}) custom-call(s32[8,128]{1,0:T(8,128)} %get-tuple-element.195.refs_4_.table_ref, f32[3136,128]{1,0:T(8,128)} %collective-permute-done.25.refs_0_, f32[4032,128]{1,0:T(8,128)} %get-tuple-element.215.refs_1_), custom_call_target="tpu_custom_call" | custom-call | tf_op jit(solution)/shard_map/cut_pieces/pallas_call | solution.py:573
  134.6 1.2 collective-permute-start.32
  135.8 29.1 %integrate_columns.4 = (f32[3584,128]{1,0:T(8,128)}, f32[3584,128]{1,0:T(8,128)}, f32[1792,128]{1,0:T(8,128)}, f32[1792,128]{1,0:T(8,128)}, f32[1792,128]{1,0:T(8,128)}) custom-call(s32[8,128]{1,0:T(8,128)} %get-tuple-element.195.refs_4_.table_ref, f32[224,1]{1,0:T(8,128)} %copy.7.loss_ref, bf16[224,224]{1,0:T(8,128)(2,1)} %pad.9.coupling_ref, ...), custom_call_target="tpu_custom_call" | custom-call | tf_op jit(solution)/shard_map/integrate_columns/pallas_call | solution.py:467
  165.0 6.9 %collective-permute-done.26.refs_0_ = f32[3584,128]{1,0:T(8,128)} collective-permute-done((f32[3584,128]{1,0:T(8,128)}, f32[3584,128]{1,0:T(8,128)}, u32[]{:S(2)}, u32[]{:S(2)}) %collective-permute-start.26) | collective-permute-done | bytes 1835040 | tf_op jit(solution)/shard_map/ppermute | solution.py:22
  171.9 24.2 %conditional.4 = (f32[3584,128]{1,0:T(8,128)}) conditional(s32[]{:T(128)} %clamp.10, f32[3584,128]{1,0:T(8,128)} %get-tuple-element.178, f32[3584,128]{1,0:T(8,128)} %get-tuple-element.178, f32[3584,128]{1,0:T(8,128)} %get-tuple-element.178, f32[3584,128]{1,0:T(8,128)} %get-tuple-element.178, ...), branch_computations={%region_10.11_spmd, %region_11.12_spmd, %region_12.13_spmd, %regio... | conditional | bytes 27525224 | solution.py:509
  171.9 1.4 slice.61
  173.3 21.5 %collective-permute-done.14 = f32[1792,128]{1,0:T(8,128)S(1)} collective-permute-done((f32[1792,128]{1,0:T(8,128)S(1)}, f32[1792,128]{1,0:T(8,128)S(1)}, u32[]{:S(2)}, u32[]{:S(2)}) %collective-permute-start.14) | collective-permute-done | bytes 917536 | tf_op jit(solution)/shard_map/cond/branch_4_fun/ppermute | solution.py:22
  194.9 1.2 copy-done.20
  197.1 4.6 %cut_pieces.3 = (f32[1792,128]{1,0:T(8,128)}, f32[1792,128]{1,0:T(8,128)}, f32[1792,128]{1,0:T(8,128)}, f32[1792,128]{1,0:T(8,128)}) custom-call(s32[8,128]{1,0:T(8,128)} %get-tuple-element.195.refs_4_.table_ref, f32[3584,128]{1,0:T(8,128)} %collective-permute-done.26.refs_0_, f32[3584,128]{1,0:T(8,128)} %get-tuple-element.216.refs_1_), custom_call_target="tpu_custom_call" | custom-call | tf_op jit(solution)/shard_map/cut_pieces/pallas_call | solution.py:573
  202.2 1.2 collective-permute-start.35
  203.5 23.9 %integrate_columns.5 = (f32[1792,128]{1,0:T(8,128)}, f32[1792,128]{1,0:T(8,128)}, f32[1792,128]{1,0:T(8,128)}, f32[1792,128]{1,0:T(8,128)}) custom-call(s32[8,128]{1,0:T(8,128)} %get-tuple-element.195.refs_4_.table_ref, f32[224,1]{1,0:T(8,128)} %copy.7.loss_ref, bf16[224,224]{1,0:T(8,128)(2,1)} %pad.9.coupling_ref, ...), custom_call_target="tpu_custom_call" | custom-call | tf_op jit(solution)/shard_map/integrate_columns/pallas_call | solution.py:467
  227.4 7.7 %collective-permute-done.36.refs_12_ = f32[3584,128]{1,0:T(8,128)} collective-permute-done((f32[3584,128]{1,0:T(8,128)}, f32[3584,128]{1,0:T(8,128)}, u32[]{:S(2)}, u32[]{:S(2)}) %collective-permute-start.36) | collective-permute-done | bytes 1835040 | tf_op jit(solution)/shard_map/ppermute | solution.py:22
  235.1 9.8 %collective-permute-done.35.refs_7_ = f32[1792,128]{1,0:T(8,128)} collective-permute-done((f32[1792,128]{1,0:T(8,128)}, f32[1792,128]{1,0:T(8,128)}, u32[]{:S(2)}, u32[]{:S(2)}) %collective-permute-start.35) | collective-permute-done | bytes 917536 | tf_op jit(solution)/shard_map/ppermute | solution.py:22
  244.9 9.4 %place_columns.1 = f32[221,4,2048]{2,1,0:T(4,128)} custom-call(s32[8,128]{1,0:T(8,128)} %get-tuple-element.195.refs_4_.table_ref, f32[1792,128]{1,0:T(8,128)} %get-tuple-element.172.refs_0_, f32[1792,128]{1,0:T(8,128)} %get-tuple-element.173.refs_1_, f32[1792,128]{1,0:T(8,128)} %get-tuple-element.174.refs_2_, f32[1792,128]{1,0:T(8,128)} %get-tuple-element.175.refs_3_, ...), custom_call_target="tpu_custom_call" | custom-call | tf_op jit(solution)/shard_map/place_columns/pallas_call | solution.py:597
  (31 shorter events, 5.2 us)
Async XLA Ops:
  0.0 20.6 %copy-start.25 = (f32[221]{0:T(256)S(1)}, f32[221]{0:T(256)}, u32[]{:S(2)}) copy-start(f32[221]{0:T(256)} %param.36) | copy-start | bytes 2656
  11.1 73.9 %collective-permute-start.25 = (f32[3136,128]{1,0:T(8,128)}, f32[3136,128]{1,0:T(8,128)}, u32[]{:S(2)}, u32[]{:S(2)}) collective-permute-start(f32[3136,128]{1,0:T(8,128)} %get-tuple-element.139), channel_id=1, source_target_pairs={{0,2},{1,3},{2,0},{3,1},{4,6},{5,7},{6,4},{7,5},{8,10},{9,11},{10,... | collective-permute-start | bytes 4816904 | tf_op jit(solution)/shard_map/ppermute | solution.py:22
  15.2 118.8 %collective-permute-start.27 = (f32[3584,128]{1,0:T(8,128)}, f32[3584,128]{1,0:T(8,128)}, u32[]{:S(2)}, u32[]{:S(2)}) collective-permute-start(f32[3584,128]{1,0:T(8,128)} %get-tuple-element.159), channel_id=1, source_target_pairs={{0,28},{4,0},{8,4},{12,8},{16,12},{20,16},{24,20},{28,24},{1,29},{... | collective-permute-start | bytes 5505032 | tf_op jit(solution)/shard_map/ppermute | solution.py:22
  16.8 117.2 %collective-permute-start.28 = (f32[3584,128]{1,0:T(8,128)}, f32[3584,128]{1,0:T(8,128)}, u32[]{:S(2)}, u32[]{:S(2)}) collective-permute-start(f32[3584,128]{1,0:T(8,128)} %get-tuple-element.160), channel_id=1, source_target_pairs={{0,4},{4,8},{8,12},{12,16},{16,20},{20,24},{24,28},{28,0},{1,5},{5... | collective-permute-start | bytes 5505032 | tf_op jit(solution)/shard_map/ppermute | solution.py:22
  16.8 117.2 %collective-permute-start.29 = (f32[3584,128]{1,0:T(8,128)}, f32[3584,128]{1,0:T(8,128)}, u32[]{:S(2)}, u32[]{:S(2)}) collective-permute-start(f32[3584,128]{1,0:T(8,128)} %get-tuple-element.161), channel_id=1, source_target_pairs={{0,8},{4,12},{8,16},{12,20},{16,24},{20,28},{24,0},{28,4},{1,9},{5... | collective-permute-start | bytes 5505032 | tf_op jit(solution)/shard_map/ppermute | solution.py:22
  21.4 10.6 %copy-start.24 = (bf16[221,221]{1,0:T(8,128)(2,1)S(1)}, bf16[221,221]{1,0:T(8,128)(2,1)}, u32[]{:S(2)}) copy-start(bf16[221,221]{1,0:T(8,128)(2,1)} %param.37) | copy-start | bytes 293050
  86.3 42.2 %collective-permute-start.6 = (f32[1792,128]{1,0:T(8,128)S(1)}, f32[1792,128]{1,0:T(8,128)S(1)}, u32[]{:S(2)}, u32[]{:S(2)}) collective-permute-start(f32[1792,128]{1,0:T(8,128)S(1)} %slice.53), channel_id=1, source_target_pairs={{0,2},{1,3},{2,0},{3,1},{4,6},{5,7},{6,4},{7,5},{8,10},{9,11},{10,... | collective-permute-start | bytes 2752520 | tf_op jit(solution)/shard_map/cond/branch_4_fun/ppermute | solution.py:22
  129.5 42.4 %collective-permute-start.26 = (f32[3584,128]{1,0:T(8,128)}, f32[3584,128]{1,0:T(8,128)}, u32[]{:S(2)}, u32[]{:S(2)}) collective-permute-start(f32[3584,128]{1,0:T(8,128)} %get-tuple-element.152), channel_id=1, source_target_pairs={{0,1},{1,2},{2,3},{3,0},{4,5},{5,6},{6,7},{7,4},{8,9},{9,10},{10,1... | collective-permute-start | bytes 5505032 | tf_op jit(solution)/shard_map/ppermute | solution.py:22
  134.0 67.6 %collective-permute-start.30 = (f32[1792,128]{1,0:T(8,128)}, f32[1792,128]{1,0:T(8,128)}, u32[]{:S(2)}, u32[]{:S(2)}) collective-permute-start(f32[1792,128]{1,0:T(8,128)} %get-tuple-element.187), channel_id=1, source_target_pairs={{0,28},{4,0},{8,4},{12,8},{16,12},{20,16},{24,20},{28,24},{1,29},{... | collective-permute-start | bytes 2752520 | tf_op jit(solution)/shard_map/ppermute | solution.py:22
  134.1 67.6 %collective-permute-start.31 = (f32[1792,128]{1,0:T(8,128)}, f32[1792,128]{1,0:T(8,128)}, u32[]{:S(2)}, u32[]{:S(2)}) collective-permute-start(f32[1792,128]{1,0:T(8,128)} %get-tuple-element.188), channel_id=1, source_target_pairs={{0,4},{4,8},{8,12},{12,16},{16,20},{20,24},{24,28},{28,0},{1,5},{5... | collective-permute-start | bytes 2752520 | tf_op jit(solution)/shard_map/ppermute | solution.py:22
  134.6 67.1 %collective-permute-start.32 = (f32[1792,128]{1,0:T(8,128)}, f32[1792,128]{1,0:T(8,128)}, u32[]{:S(2)}, u32[]{:S(2)}) collective-permute-start(f32[1792,128]{1,0:T(8,128)} %get-tuple-element.189), channel_id=1, source_target_pairs={{0,8},{4,12},{8,16},{12,20},{16,24},{20,28},{24,0},{28,4},{1,9},{5... | collective-permute-start | bytes 2752520 | tf_op jit(solution)/shard_map/ppermute | solution.py:22
  171.9 23.0 %copy-start.16 = (f32[3584,128]{1,0:T(8,128)S(1)}, f32[3584,128]{1,0:T(8,128)}, u32[]{:S(2)}) copy-start(f32[3584,128]{1,0:T(8,128)} %param.14) | copy-start | bytes 5505028 | tf_op jit(solution)/shard_map/cond
  173.3 21.6 %collective-permute-start.14 = (f32[1792,128]{1,0:T(8,128)S(1)}, f32[1792,128]{1,0:T(8,128)S(1)}, u32[]{:S(2)}, u32[]{:S(2)}) collective-permute-start(f32[1792,128]{1,0:T(8,128)S(1)} %slice.61), channel_id=1, source_target_pairs={{0,1},{1,2},{2,3},{3,0},{4,5},{5,6},{6,7},{7,4},{8,9},{9,10},{10,1... | collective-permute-start | bytes 2752520 | tf_op jit(solution)/shard_map/cond/branch_4_fun/ppermute | solution.py:22
  194.9 1.2 copy-start.20
  196.1 39.0 %collective-permute-start.36 = (f32[3584,128]{1,0:T(8,128)}, f32[3584,128]{1,0:T(8,128)}, u32[]{:S(2)}, u32[]{:S(2)}) collective-permute-start(f32[3584,128]{1,0:T(8,128)} %get-tuple-element.194), channel_id=1, source_target_pairs={{0,3},{1,0},{2,1},{3,2},{4,7},{5,4},{6,5},{7,6},{8,11},{9,8},{10,9... | collective-permute-start | bytes 5505032 | tf_op jit(solution)/shard_map/ppermute | solution.py:22
  201.7 33.4 %collective-permute-start.33 = (f32[1792,128]{1,0:T(8,128)}, f32[1792,128]{1,0:T(8,128)}, u32[]{:S(2)}, u32[]{:S(2)}) collective-permute-start(f32[1792,128]{1,0:T(8,128)} %get-tuple-element.190), channel_id=1, source_target_pairs={{0,28},{4,0},{8,4},{12,8},{16,12},{20,16},{24,20},{28,24},{1,29},{... | collective-permute-start | bytes 2752520 | tf_op jit(solution)/shard_map/ppermute | solution.py:22
  201.7 33.3 %collective-permute-start.34 = (f32[1792,128]{1,0:T(8,128)}, f32[1792,128]{1,0:T(8,128)}, u32[]{:S(2)}, u32[]{:S(2)}) collective-permute-start(f32[1792,128]{1,0:T(8,128)} %get-tuple-element.192), channel_id=1, source_target_pairs={{0,4},{4,8},{8,12},{12,16},{16,20},{20,24},{24,28},{28,0},{1,5},{5... | collective-permute-start | bytes 2752520 | tf_op jit(solution)/shard_map/ppermute | solution.py:22
  202.2 42.7 %collective-permute-start.35 = (f32[1792,128]{1,0:T(8,128)}, f32[1792,128]{1,0:T(8,128)}, u32[]{:S(2)}, u32[]{:S(2)}) collective-permute-start(f32[1792,128]{1,0:T(8,128)} %get-tuple-element.193), channel_id=1, source_target_pairs={{0,8},{4,12},{8,16},{12,20},{16,24},{20,28},{24,0},{28,4},{1,9},{5... | collective-permute-start | bytes 2752520 | tf_op jit(solution)/shard_map/ppermute | solution.py:22
where the time goes:
time: 258 us; the launch traced here: 255 us
  waiting for transfers between devices  119 us (46%)
  Pallas kernels  115 us (45%)
  starting transfers between devices  10.8 us (4%)
  local copies, waits for them, and re-layouts  7.85 us (3%)
    ppermute x14, waiting for transfers between devices, from_behind(): return lax.ppermute(value, axis, pairs)  119 us
    pallas_call x3, Pallas kernels, integrate(): pl.pallas_call(functools.partial(integrate_kernel, (levels, pad, tiles),...  74.6 us
    pallas_call x2, Pallas kernels, sort(): pl.pallas_call(functools.partial(sort_kernel, (species, levels, columns,...  21.7 us
    ppermute x14, starting transfers between devices, from_behind(): return lax.ppermute(value, axis, pairs)  10.8 us
    pallas_call x1, Pallas kernels, local(): pl.pallas_call(functools.partial(finish_kernel, (species, levels, columns...  9.43 us
    pallas_call x2, Pallas kernels, local(): pl.pallas_call(functools.partial(cut_kernel, static, tiles, piece, step),...  9.08 us
  transfers between devices with their start and end apart: 14, of which 6 were waited for; matrix products, arithmetic and copies ran while one was open for 3% of the time, Pallas kernels for 37%

commit v1 on v0

--- a/solution.py
+++ b/solution.py
@@ -128,12 +128,14 @@
     waits = []
     quarter = static // 4
     for part in range(4):
-        span = span_of(part * quarter, quarter, tiles)
-        copy = pltpu.make_async_copy(refs[0].at[span], room_ref.at[span], sem_ref.at[part])
+        copy = pltpu.make_async_copy(
+            refs[part // 2].at[span_of(part % 2 * quarter, quarter, tiles)],
+            room_ref.at[span_of(part * quarter, quarter, tiles)], sem_ref.at[part],
+        )
         copy.start()
         waits.append((None, copy))
     copy = pltpu.make_async_copy(
-        refs[1], room_ref.at[pl.ds(static * 8 * tiles, refs[1].shape[0])], sem_ref.at[4]
+        refs[2], room_ref.at[pl.ds(static * 8 * tiles, refs[2].shape[0])], sem_ref.at[4]
     )
     pl.when(in_step > static)(copy.start)
     waits.append((in_step > static, copy))
@@ -259,9 +261,9 @@
 
 
 def cut_kernel(static, tiles, piece, step, table_ref, *refs):
-    pieces = refs[2:2 + WIN]
-    room_ref, sem_ref, out_sem = refs[2 + WIN:]
-    wait_all(start_arrival(refs[:2], sem_ref, room_ref, table_ref[3, step * WIN], static, tiles))
+    pieces = refs[3:3 + WIN]
+    room_ref, sem_ref, out_sem = refs[3 + WIN:]
+    wait_all(start_arrival(refs[:3], sem_ref, room_ref, table_ref[3, step * WIN], static, tiles))
     copies = []
     quarter = piece // 4
     for at in range(WIN):
@@ -297,7 +299,7 @@
             pl.when(wanted)(copy.start)
             parts.append((wanted, copy))
         copies.append(parts)
-    waits = start_arrival(refs[whole_pieces:whole_pieces + 2], room_sem, room_ref,
+    waits = start_arrival(refs[whole_pieces:whole_pieces + 3], room_sem, room_ref,
                           table_ref[3, whole_pieces], static, tiles)
     lane = lax.broadcasted_iota(jnp.int32, (1, LANES), 1)
     in_group = lax.broadcasted_iota(jnp.int32, (8, LANES), 0)
@@ -437,11 +439,16 @@
         )
 
     first_static = statics[order[0]]
-    cuts = [(0, 0, entry(1, order[0]), first_static, entry(3, order[0]))]
+    half = first_static // 2
+    cuts = [
+        (0, 0, entry(1, order[0]), half, entry(3, order[0])),
+        (1, 0, lambda table: entry(1, order[0])(table) + half, half,
+         lambda table: entry(3, order[0])(table) - half),
+    ]
     for index, at in enumerate(moving):
-        cuts += pair_cuts(1 + index, at)
+        cuts += pair_cuts(2 + index, at)
     table, places, *first = sort(
-        cuts, [first_static] + [2 * piece] * len(moving), True, ()
+        cuts, [half, half] + [2 * piece] * len(moving), True, ()
     )
     cuts = [(0, 0, over(order[0]), most - first_static, groups_over(order[0]))]
     cuts += pair_cuts(1, 1)
@@ -502,17 +509,23 @@
         def leaf(units, rest):
             if units == 0:
                 return rest
-            got = from_behind(rest[:units * UNIT * 8 * tiles], "narrow", step)
-            return lax.dynamic_update_slice(rest, got, (0, 0))
+            half = units * UNIT * 4 * tiles
+            both = [
+                from_behind(rest[part * half:(part + 1) * half], "narrow", step)
+                for part in range(2)
+            ]
+            for part in range(2):
+                rest = lax.dynamic_update_slice(rest, both[part], (part * half, 0))
+            return rest
 
         leaves = [functools.partial(leaf, count) for count in range((most - statics[step]) // UNIT + 1)]
         return lax.switch(units, leaves, rest)
 
     pieces = {}
-    outgoing = [first[0], first_rest]
-    wide_now = first[1:]
+    outgoing = [first[0], first[1], first_rest]
+    wide_now = first[2:]
     keys_now = [[(at, 0), (at, last)] for at in moving]
-    static_part = from_behind(outgoing[0], "narrow", order[0])
+    static_part = [from_behind(value, "narrow", order[0]) for value in outgoing[:2]]
     wide_got = [from_behind(value, "wide", at - 1) for value, at in zip(wide_now, moving)]
     table_then = table
     for phase, step in enumerate(order):
@@ -536,7 +549,9 @@
                 loads.append((0, None, most, 0))
                 used = most
             blocks += group_blocks(0, coming)
-            stores += [(here(0), statics[coming]), (here(statics[coming]), most - statics[coming])]
+            half = statics[coming] // 2
+            stores += [(here(0), half), (here(half), half)]
+            stores += [(here(statics[coming]), most - statics[coming])]
         extra = []
         if phase == 0:
             extra.append(((1, 0), (local_rows, 0)))
@@ -556,7 +571,7 @@
             results = integrate(table_then, operands, loads, merges, blocks, stores)
         else:
             results = []
-        rest = outgoing[1]
+        rest = outgoing[2]
         if phase == 0:
             static_part, results, rest, units = lax.optimization_barrier(
                 (static_part, results, rest, units)
@@ -565,10 +580,12 @@
             static_part, results, rest = lax.optimization_barrier((static_part, results, rest))
         done = {key: (value, 0) for key, value in zip(named, results[len(results) - len(named):])}
         outgoing = results[:len(results) - len(named)]
-        arrived = [static_part, step_over(step, units[phase], rest)]
+        arrived = list(static_part) + [step_over(step, units[phase], rest)]
         if step != last:
             arrived, outgoing = lax.optimization_barrier((arrived, outgoing))
-            static_part = from_behind(outgoing[0], "narrow", order[phase + 1])
+            static_part = [
+                from_behind(value, "narrow", order[phase + 1]) for value in outgoing[:2]
+            ]
         if step != last:
             cut = pl.pallas_call(
                 functools.partial(cut_kernel, static, tiles, piece, step),

time: 258 us -> 234 us (0.907)
  waiting for transfers between devices: 119 us -> 99.9 us
  Pallas kernels: 115 us -> 111 us
    ppermute x14 -> x19, waiting for transfers between devices: 119 us -> 99.9 us  [from_behind(): return lax.ppermute(value, axis, pairs)]
    pallas_call x3, Pallas kernels: 74.6 us -> 70.6 us  [integrate(): pl.pallas_call(functools.partial(integrate_kernel, (levels, pad, tiles),...]
    slice x2 -> x4, local copies, waits for them, and re-layouts: 2.61 us -> 5.28 us  [leaf(): rest[part * half:(part + 1) * half]]
    ppermute x14 -> x19, starting transfers between devices: 10.8 us -> 8.6 us  [from_behind(): return lax.ppermute(value, axis, pairs)]
  transfers between devices with their start and end apart: 14 -> 19, of which waited for: 6 -> 9; matrix products, arithmetic and copies ran while one was open for 3% -> 4% of each run, Pallas kernels for 37% -> 39%
where the time goes in v1:
time: 234 us; the launch traced here: 231 us
  Pallas kernels  111 us (47%)
  waiting for transfers between devices  99.9 us (43%)
  local copies, waits for them, and re-layouts  9.53 us (4%)
  starting transfers between devices  8.6 us (4%)
    ppermute x19, waiting for transfers between devices, from_behind(): return lax.ppermute(value, axis, pairs)  99.9 us
    pallas_call x3, Pallas kernels, integrate(): pl.pallas_call(functools.partial(integrate_kernel, (levels, pad, tiles),...  70.6 us
    pallas_call x2, Pallas kernels, sort(): pl.pallas_call(functools.partial(sort_kernel, (species, levels, columns,...  21.9 us
    pallas_call x1, Pallas kernels, local(): pl.pallas_call(functools.partial(finish_kernel, (species, levels, columns...  9.36 us
    pallas_call x2, Pallas kernels, local(): pl.pallas_call(functools.partial(cut_kernel, static, tiles, piece, step),...  8.88 us
    ppermute x19, starting transfers between devices, from_behind(): return lax.ppermute(value, axis, pairs)  8.6 us
    slice x4, local copies, waits for them, and re-layouts, leaf(): rest[part * half:(part + 1) * half]  5.28 us
  transfers between devices with their start and end apart: 19, of which 9 were waited for; matrix products, arithmetic and copies ran while one was open for 4% of the time, Pallas kernels for 39%

profile of v1, /device:TPU:0, one launch (start us, length us, event | category | flops | bytes accessed | tf_op | source)
XLA Modules:
  0.0 231.0 jit_solution(11612844656750298351)
XLA Ops:
  0.0 11.4 %sort_columns.1 = (s32[8,128]{1,0:T(8,128)}, s32[1,2048]{1,0:T(1,128)}, f32[1568,128]{1,0:T(8,128)}, f32[1568,128]{1,0:T(8,128)}, f32[3584,128]{1,0:T(8,128)}, /*index=5*/f32[3584,128]{1,0:T(8,128)}, f32[3584,128]{1,0:T(8,128)}) custom-call(s32[1,2048]{1,0:T(1,128)} %bitcast.11, f32[1,2048]{1,0:T(1,128)} %bitcast.13, s32[1,2048]{1,0:T(1,128)} %bitcast.15, ...), custom_call_target="tpu_custom_call" | custom-call | tf_op jit(solution)/shard_map/sort_columns/pallas_call | solution.py:410
  11.4 3.4 %collective-permute-start.54 = (f32[3584,128]{1,0:T(8,128)}, f32[3584,128]{1,0:T(8,128)}, u32[]{:S(2)}, u32[]{:S(2)}) collective-permute-start(f32[3584,128]{1,0:T(8,128)} %get-tuple-element.177), channel_id=1, source_target_pairs={{0,28},{4,0},{8,4},{12,8},{16,12},{20,16},{24,20},{28,24},{1,29},{... | collective-permute-start | bytes 5505032 | tf_op jit(solution)/shard_map/ppermute | solution.py:22
  14.9 2.6 %collective-permute-start.50 = (f32[1568,128]{1,0:T(8,128)}, f32[1568,128]{1,0:T(8,128)}, u32[]{:S(2)}, u32[]{:S(2)}) collective-permute-start(f32[1568,128]{1,0:T(8,128)} %get-tuple-element.151), channel_id=1, source_target_pairs={{0,2},{1,3},{2,0},{3,1},{4,6},{5,7},{6,4},{7,5},{8,10},{9,11},{10,... | collective-permute-start | bytes 2408456 | tf_op jit(solution)/shard_map/ppermute | solution.py:22
  17.9 1.4 fusion.25
  21.9 10.5 %sort_later_columns.1 = (f32[4032,128]{1,0:T(8,128)}, f32[3584,128]{1,0:T(8,128)}, f32[7168,128]{1,0:T(8,128)}) custom-call(s32[1,2048]{1,0:T(1,128)} %bitcast.12, f32[1,2048]{1,0:T(1,128)} %bitcast.14, s32[1,2048]{1,0:T(1,128)} %bitcast.16, f32[221,4,2048]{2,1,0:T(4,128)} %bitcast.10, s32[8,128]{1,0:T(8,128)} %get-tuple-element.218.refs_4_.table_ref, ...), custom_call_target="tpu_custom_call" | custom-call | tf_op jit(solution)/shard_map/sort_later_columns/pallas_call | solution.py:410
  33.1 21.5 %integrate_columns.3 = (f32[1792,128]{1,0:T(8,128)}, f32[1792,128]{1,0:T(8,128)}, f32[3584,128]{1,0:T(8,128)}, f32[1792,128]{1,0:T(8,128)}) custom-call(s32[8,128]{1,0:T(8,128)} %get-tuple-element.218.refs_4_.table_ref, f32[224,1]{1,0:T(8,128)} %copy.7.loss_ref, bf16[224,224]{1,0:T(8,128)(2,1)} %pad.9.coupling_ref, f32[7168,128]{1,0:T(8,128)} %get-tuple-element.154.refs_0_, ...), custom_call_target="tpu_custom_call" | custom-call | tf_op jit(solution)/shard_map/integrate_columns/pallas_call | solution.py:474
  54.6 16.0 %collective-permute-done.50.refs_0_ = f32[1568,128]{1,0:T(8,128)} collective-permute-done((f32[1568,128]{1,0:T(8,128)}, f32[1568,128]{1,0:T(8,128)}, u32[]{:S(2)}, u32[]{:S(2)}) %collective-permute-start.50) | collective-permute-done | bytes 802848 | tf_op jit(solution)/shard_map/ppermute | solution.py:22
  70.6 17.2 %collective-permute-done.51.refs_1_ = f32[1568,128]{1,0:T(8,128)} collective-permute-done((f32[1568,128]{1,0:T(8,128)}, f32[1568,128]{1,0:T(8,128)}, u32[]{:S(2)}, u32[]{:S(2)}) %collective-permute-start.51) | collective-permute-done | bytes 802848 | tf_op jit(solution)/shard_map/ppermute | solution.py:22
  87.8 19.0 %conditional.3 = (f32[4032,128]{1,0:T(8,128)}) conditional(s32[]{:T(128)} %clamp.9, f32[4032,128]{1,0:T(8,128)} %get-tuple-element.164, f32[4032,128]{1,0:T(8,128)} %get-tuple-element.164, f32[4032,128]{1,0:T(8,128)} %get-tuple-element.164, f32[4032,128]{1,0:T(8,128)} %get-tuple-element.164, ...), branch_computations={%region_0.1_spmd, %region_1.2_spmd, %region_2.3_spmd, %region_3.4_... | conditional | bytes 33030288 | solution.py:522
  88.8 9.2 %collective-permute-done = f32[224,128]{1,0:T(8,128)S(1)} collective-permute-done((f32[224,128]{1,0:T(8,128)S(1)}, f32[224,128]{1,0:T(8,128)S(1)}, u32[]{:S(2)}, u32[]{:S(2)}) %collective-permute-start) | collective-permute-done | bytes 114720 | tf_op jit(solution)/shard_map/cond/branch_1_fun/ppermute | solution.py:22
  98.0 1.6 fusion
  99.5 6.6 %collective-permute-done.1 = f32[224,128]{1,0:T(8,128)S(1)} collective-permute-done((f32[224,128]{1,0:T(8,128)S(1)}, f32[224,128]{1,0:T(8,128)S(1)}, u32[]{:S(2)}, u32[]{:S(2)}) %collective-permute-start.1) | collective-permute-done | bytes 114720 | tf_op jit(solution)/shard_map/cond/branch_1_fun/ppermute | solution.py:22
  107.0 4.3 %cut_pieces.2 = (f32[1792,128]{1,0:T(8,128)}, f32[1792,128]{1,0:T(8,128)}, f32[1792,128]{1,0:T(8,128)}, f32[1792,128]{1,0:T(8,128)}) custom-call(s32[8,128]{1,0:T(8,128)} %get-tuple-element.218.refs_4_.table_ref, f32[1568,128]{1,0:T(8,128)} %collective-permute-done.50.refs_0_, f32[1568,128]{1,0:T(8,128)} %collective-permute-done.51.refs_1_, ...), custom_call_target="tpu_custom_call" | custom-call | tf_op jit(solution)/shard_map/cut_pieces/pallas_call | solution.py:590
  112.7 26.0 %integrate_columns.4 = (f32[1792,128]{1,0:T(8,128)}, f32[1792,128]{1,0:T(8,128)}, f32[3584,128]{1,0:T(8,128)}, f32[1792,128]{1,0:T(8,128)}, f32[1792,128]{1,0:T(8,128)}, /*index=5*/f32[1792,128]{1,0:T(8,128)}) custom-call(s32[8,128]{1,0:T(8,128)} %get-tuple-element.218.refs_4_.table_ref, f32[224,1]{1,0:T(8,128)} %copy.7.loss_ref, ...), custom_call_target="tpu_custom_call" | custom-call | tf_op jit(solution)/shard_map/integrate_columns/pallas_call | solution.py:474
  138.7 12.0 %collective-permute-done.53.refs_1_ = f32[1792,128]{1,0:T(8,128)} collective-permute-done((f32[1792,128]{1,0:T(8,128)}, f32[1792,128]{1,0:T(8,128)}, u32[]{:S(2)}, u32[]{:S(2)}) %collective-permute-start.53) | collective-permute-done | bytes 917536 | tf_op jit(solution)/shard_map/ppermute | solution.py:22
  150.7 25.6 %conditional.4 = (f32[3584,128]{1,0:T(8,128)}) conditional(s32[]{:T(128)} %clamp.10, f32[3584,128]{1,0:T(8,128)} %get-tuple-element.198, f32[3584,128]{1,0:T(8,128)} %get-tuple-element.198, f32[3584,128]{1,0:T(8,128)} %get-tuple-element.198, f32[3584,128]{1,0:T(8,128)} %get-tuple-element.198, ...), branch_computations={%region_10.11_spmd, %region_11.12_spmd, %region_12.13_spmd, %regio... | conditional | bytes 29360272 | solution.py:522
  151.8 10.7 %collective-permute-done.22 = f32[672,128]{1,0:T(8,128)S(1)} collective-permute-done((f32[672,128]{1,0:T(8,128)S(1)}, f32[672,128]{1,0:T(8,128)S(1)}, u32[]{:S(2)}, u32[]{:S(2)}) %collective-permute-start.22) | collective-permute-done | bytes 344096 | tf_op jit(solution)/shard_map/cond/branch_3_fun/ppermute | solution.py:22
  162.5 1.8 fusion.11
  164.3 11.3 %collective-permute-done.23 = f32[672,128]{1,0:T(8,128)S(1)} collective-permute-done((f32[672,128]{1,0:T(8,128)S(1)}, f32[672,128]{1,0:T(8,128)S(1)}, u32[]{:S(2)}, u32[]{:S(2)}) %collective-permute-start.23) | collective-permute-done | bytes 344096 | tf_op jit(solution)/shard_map/cond/branch_3_fun/ppermute | solution.py:22
  176.3 4.6 %cut_pieces.3 = (f32[1792,128]{1,0:T(8,128)}, f32[1792,128]{1,0:T(8,128)}, f32[1792,128]{1,0:T(8,128)}, f32[1792,128]{1,0:T(8,128)}) custom-call(s32[8,128]{1,0:T(8,128)} %get-tuple-element.218.refs_4_.table_ref, f32[1792,128]{1,0:T(8,128)} %collective-permute-done.52.refs_0_, f32[1792,128]{1,0:T(8,128)} %collective-permute-done.53.refs_1_, ...), custom_call_target="tpu_custom_call" | custom-call | tf_op jit(solution)/shard_map/cut_pieces/pallas_call | solution.py:590
  181.4 23.1 %integrate_columns.5 = (f32[1792,128]{1,0:T(8,128)}, f32[1792,128]{1,0:T(8,128)}, f32[1792,128]{1,0:T(8,128)}, f32[1792,128]{1,0:T(8,128)}) custom-call(s32[8,128]{1,0:T(8,128)} %get-tuple-element.218.refs_4_.table_ref, f32[224,1]{1,0:T(8,128)} %copy.7.loss_ref, bf16[224,224]{1,0:T(8,128)(2,1)} %pad.9.coupling_ref, ...), custom_call_target="tpu_custom_call" | custom-call | tf_op jit(solution)/shard_map/integrate_columns/pallas_call | solution.py:474
  204.5 10.0 %collective-permute-done.64.refs_13_ = f32[1792,128]{1,0:T(8,128)} collective-permute-done((f32[1792,128]{1,0:T(8,128)}, f32[1792,128]{1,0:T(8,128)}, u32[]{:S(2)}, u32[]{:S(2)}) %collective-permute-start.64) | collective-permute-done | bytes 917536 | tf_op jit(solution)/shard_map/ppermute | solution.py:22
  214.6 6.9 %collective-permute-done.62.refs_7_ = f32[1792,128]{1,0:T(8,128)} collective-permute-done((f32[1792,128]{1,0:T(8,128)}, f32[1792,128]{1,0:T(8,128)}, u32[]{:S(2)}, u32[]{:S(2)}) %collective-permute-start.62) | collective-permute-done | bytes 917536 | tf_op jit(solution)/shard_map/ppermute | solution.py:22
  221.5 9.4 %place_columns.1 = f32[221,4,2048]{2,1,0:T(4,128)} custom-call(s32[8,128]{1,0:T(8,128)} %get-tuple-element.218.refs_4_.table_ref, f32[1792,128]{1,0:T(8,128)} %get-tuple-element.191.refs_0_, f32[1792,128]{1,0:T(8,128)} %get-tuple-element.192.refs_1_, f32[1792,128]{1,0:T(8,128)} %get-tuple-element.193.refs_2_, f32[1792,128]{1,0:T(8,128)} %get-tuple-element.194.refs_3_, ...), custom_call_target="tpu_custom_call" | custom-call | tf_op jit(solution)/shard_map/place_columns/pallas_call | solution.py:614
  (39 shorter events, 7.4 us)
Async XLA Ops:
  0.0 21.1 %copy-start.7 = (f32[221]{0:T(256)S(1)}, f32[221]{0:T(256)}, u32[]{:S(2)}) copy-start(f32[221]{0:T(256)} %param.36) | copy-start | bytes 2656
  11.4 99.9 %collective-permute-start.54 = (f32[3584,128]{1,0:T(8,128)}, f32[3584,128]{1,0:T(8,128)}, u32[]{:S(2)}, u32[]{:S(2)}) collective-permute-start(f32[3584,128]{1,0:T(8,128)} %get-tuple-element.177), channel_id=1, source_target_pairs={{0,28},{4,0},{8,4},{12,8},{16,12},{20,16},{24,20},{28,24},{1,29},{... | collective-permute-start | bytes 5505032 | tf_op jit(solution)/shard_map/ppermute | solution.py:22
  14.8 96.6 %collective-permute-start.55 = (f32[3584,128]{1,0:T(8,128)}, f32[3584,128]{1,0:T(8,128)}, u32[]{:S(2)}, u32[]{:S(2)}) collective-permute-start(f32[3584,128]{1,0:T(8,128)} %get-tuple-element.178), channel_id=1, source_target_pairs={{0,4},{4,8},{8,12},{12,16},{16,20},{20,24},{24,28},{28,0},{1,5},{5... | collective-permute-start | bytes 5505032 | tf_op jit(solution)/shard_map/ppermute | solution.py:22
  14.8 96.6 %collective-permute-start.56 = (f32[3584,128]{1,0:T(8,128)}, f32[3584,128]{1,0:T(8,128)}, u32[]{:S(2)}, u32[]{:S(2)}) collective-permute-start(f32[3584,128]{1,0:T(8,128)} %get-tuple-element.179), channel_id=1, source_target_pairs={{0,8},{4,12},{8,16},{12,20},{16,24},{20,28},{24,0},{28,4},{1,9},{5... | collective-permute-start | bytes 5505032 | tf_op jit(solution)/shard_map/ppermute | solution.py:22
  14.9 55.7 %collective-permute-start.50 = (f32[1568,128]{1,0:T(8,128)}, f32[1568,128]{1,0:T(8,128)}, u32[]{:S(2)}, u32[]{:S(2)}) collective-permute-start(f32[1568,128]{1,0:T(8,128)} %get-tuple-element.151), channel_id=1, source_target_pairs={{0,2},{1,3},{2,0},{3,1},{4,6},{5,7},{6,4},{7,5},{8,10},{9,11},{10,... | collective-permute-start | bytes 2408456 | tf_op jit(solution)/shard_map/ppermute | solution.py:22
  17.5 70.3 %collective-permute-start.51 = (f32[1568,128]{1,0:T(8,128)}, f32[1568,128]{1,0:T(8,128)}, u32[]{:S(2)}, u32[]{:S(2)}) collective-permute-start(f32[1568,128]{1,0:T(8,128)} %get-tuple-element.152), channel_id=1, source_target_pairs={{0,2},{1,3},{2,0},{3,1},{4,6},{5,7},{6,4},{7,5},{8,10},{9,11},{10,... | collective-permute-start | bytes 2408456 | tf_op jit(solution)/shard_map/ppermute | solution.py:22
  21.9 10.5 %copy-start.6 = (bf16[221,221]{1,0:T(8,128)(2,1)S(1)}, bf16[221,221]{1,0:T(8,128)(2,1)}, u32[]{:S(2)}) copy-start(bf16[221,221]{1,0:T(8,128)(2,1)} %param.37) | copy-start | bytes 293050
  88.8 9.2 %collective-permute-start = (f32[224,128]{1,0:T(8,128)S(1)}, f32[224,128]{1,0:T(8,128)S(1)}, u32[]{:S(2)}, u32[]{:S(2)}) collective-permute-start(f32[224,128]{1,0:T(8,128)S(1)} %slice.106), channel_id=1, source_target_pairs={{0,2},{1,3},{2,0},{3,1},{4,6},{5,7},{6,4},{7,5},{8,10},{9,11},{10,... | collective-permute-start | bytes 344072 | tf_op jit(solution)/shard_map/cond/branch_1_fun/ppermute | solution.py:22
  99.5 6.6 %collective-permute-start.1 = (f32[224,128]{1,0:T(8,128)S(1)}, f32[224,128]{1,0:T(8,128)S(1)}, u32[]{:S(2)}, u32[]{:S(2)}) collective-permute-start(f32[224,128]{1,0:T(8,128)S(1)} %get-tuple-element.236), channel_id=1, source_target_pairs={{0,2},{1,3},{2,0},{3,1},{4,6},{5,7},{6,4},{7,5},{8,10},{9,11},{10,... | collective-permute-start | bytes 344072 | tf_op jit(solution)/shard_map/cond/branch_1_fun/ppermute | solution.py:22
  106.8 31.9 %collective-permute-start.52 = (f32[1792,128]{1,0:T(8,128)}, f32[1792,128]{1,0:T(8,128)}, u32[]{:S(2)}, u32[]{:S(2)}) collective-permute-start(f32[1792,128]{1,0:T(8,128)} %get-tuple-element.168), channel_id=1, source_target_pairs={{0,1},{1,2},{2,3},{3,0},{4,5},{5,6},{6,7},{7,4},{8,9},{9,10},{10,1... | collective-permute-start | bytes 2752520 | tf_op jit(solution)/shard_map/ppermute | solution.py:22
  106.8 43.9 %collective-permute-start.53 = (f32[1792,128]{1,0:T(8,128)}, f32[1792,128]{1,0:T(8,128)}, u32[]{:S(2)}, u32[]{:S(2)}) collective-permute-start(f32[1792,128]{1,0:T(8,128)} %get-tuple-element.169), channel_id=1, source_target_pairs={{0,1},{1,2},{2,3},{3,0},{4,5},{5,6},{6,7},{7,4},{8,9},{9,10},{10,1... | collective-permute-start | bytes 2752520 | tf_op jit(solution)/shard_map/ppermute | solution.py:22
  111.4 69.5 %collective-permute-start.57 = (f32[1792,128]{1,0:T(8,128)}, f32[1792,128]{1,0:T(8,128)}, u32[]{:S(2)}, u32[]{:S(2)}) collective-permute-start(f32[1792,128]{1,0:T(8,128)} %get-tuple-element.209), channel_id=1, source_target_pairs={{0,28},{4,0},{8,4},{12,8},{16,12},{20,16},{24,20},{28,24},{1,29},{... | collective-permute-start | bytes 2752520 | tf_op jit(solution)/shard_map/ppermute | solution.py:22
  111.5 69.4 %collective-permute-start.58 = (f32[1792,128]{1,0:T(8,128)}, f32[1792,128]{1,0:T(8,128)}, u32[]{:S(2)}, u32[]{:S(2)}) collective-permute-start(f32[1792,128]{1,0:T(8,128)} %get-tuple-element.210), channel_id=1, source_target_pairs={{0,4},{4,8},{8,12},{12,16},{16,20},{20,24},{24,28},{28,0},{1,5},{5... | collective-permute-start | bytes 2752520 | tf_op jit(solution)/shard_map/ppermute | solution.py:22
  112.0 68.9 %collective-permute-start.59 = (f32[1792,128]{1,0:T(8,128)}, f32[1792,128]{1,0:T(8,128)}, u32[]{:S(2)}, u32[]{:S(2)}) collective-permute-start(f32[1792,128]{1,0:T(8,128)} %get-tuple-element.211), channel_id=1, source_target_pairs={{0,8},{4,12},{8,16},{12,20},{16,24},{20,28},{24,0},{28,4},{1,9},{5... | collective-permute-start | bytes 2752520 | tf_op jit(solution)/shard_map/ppermute | solution.py:22
  151.7 10.8 %collective-permute-start.22 = (f32[672,128]{1,0:T(8,128)S(1)}, f32[672,128]{1,0:T(8,128)S(1)}, u32[]{:S(2)}, u32[]{:S(2)}) collective-permute-start(f32[672,128]{1,0:T(8,128)S(1)} %slice.128), channel_id=1, source_target_pairs={{0,1},{1,2},{2,3},{3,0},{4,5},{5,6},{6,7},{7,4},{8,9},{9,10},{10,1... | collective-permute-start | bytes 1032200 | tf_op jit(solution)/shard_map/cond/branch_3_fun/ppermute | solution.py:22
  164.3 11.3 %collective-permute-start.23 = (f32[672,128]{1,0:T(8,128)S(1)}, f32[672,128]{1,0:T(8,128)S(1)}, u32[]{:S(2)}, u32[]{:S(2)}) collective-permute-start(f32[672,128]{1,0:T(8,128)S(1)} %get-tuple-element.258), channel_id=1, source_target_pairs={{0,1},{1,2},{2,3},{3,0},{4,5},{5,6},{6,7},{7,4},{8,9},{9,10},{10,1... | collective-permute-start | bytes 1032200 | tf_op jit(solution)/shard_map/cond/branch_3_fun/ppermute | solution.py:22
  176.3 28.2 %collective-permute-start.63 = (f32[1792,128]{1,0:T(8,128)}, f32[1792,128]{1,0:T(8,128)}, u32[]{:S(2)}, u32[]{:S(2)}) collective-permute-start(f32[1792,128]{1,0:T(8,128)} %get-tuple-element.216), channel_id=1, source_target_pairs={{0,3},{1,0},{2,1},{3,2},{4,7},{5,4},{6,5},{7,6},{8,11},{9,8},{10,9... | collective-permute-start | bytes 2752520 | tf_op jit(solution)/shard_map/ppermute | solution.py:22
  176.3 38.3 %collective-permute-start.64 = (f32[1792,128]{1,0:T(8,128)}, f32[1792,128]{1,0:T(8,128)}, u32[]{:S(2)}, u32[]{:S(2)}) collective-permute-start(f32[1792,128]{1,0:T(8,128)} %get-tuple-element.217), channel_id=1, source_target_pairs={{0,3},{1,0},{2,1},{3,2},{4,7},{5,4},{6,5},{7,6},{8,11},{9,8},{10,9... | collective-permute-start | bytes 2752520 | tf_op jit(solution)/shard_map/ppermute | solution.py:22
  180.9 33.7 %collective-permute-start.60 = (f32[1792,128]{1,0:T(8,128)}, f32[1792,128]{1,0:T(8,128)}, u32[]{:S(2)}, u32[]{:S(2)}) collective-permute-start(f32[1792,128]{1,0:T(8,128)} %get-tuple-element.212), channel_id=1, source_target_pairs={{0,28},{4,0},{8,4},{12,8},{16,12},{20,16},{24,20},{28,24},{1,29},{... | collective-permute-start | bytes 2752520 | tf_op jit(solution)/shard_map/ppermute | solution.py:22
  180.9 33.6 %collective-permute-start.61 = (f32[1792,128]{1,0:T(8,128)}, f32[1792,128]{1,0:T(8,128)}, u32[]{:S(2)}, u32[]{:S(2)}) collective-permute-start(f32[1792,128]{1,0:T(8,128)} %get-tuple-element.214), channel_id=1, source_target_pairs={{0,4},{4,8},{8,12},{12,16},{16,20},{20,24},{24,28},{28,0},{1,5},{5... | collective-permute-start | bytes 2752520 | tf_op jit(solution)/shard_map/ppermute | solution.py:22
  181.4 40.0 %collective-permute-start.62 = (f32[1792,128]{1,0:T(8,128)}, f32[1792,128]{1,0:T(8,128)}, u32[]{:S(2)}, u32[]{:S(2)}) collective-permute-start(f32[1792,128]{1,0:T(8,128)} %get-tuple-element.215), channel_id=1, source_target_pairs={{0,8},{4,12},{8,16},{12,20},{16,24},{20,28},{24,0},{28,4},{1,9},{5... | collective-permute-start | bytes 2752520 | tf_op jit(solution)/shard_map/ppermute | solution.py:22
